TPU v7x, 128 devices: a whole 4x4x4 slice. The times are simulated.
128 devices in a mesh: src: 4 (over z_hi, core), tgt: 32 (over y, z_lo, x).
Axes of the slice: x: 4, y: 4, z: 4 (z_hi: 2, z_lo: 2; z = z_hi * 2 + z_lo), core: 2. Of those that a mesh axis runs over, the one named last changes fastest.
Arguments:
- forward_init: float32 [256, 32768], P(None, 'src'), may hold values from 0.1 to 10
- transition: bfloat16 [32768, 32768], P('src', 'tgt'), may hold values from 0 to 2976, as said below
- emission: bfloat16 [4096, 32768], P('src', 'tgt'), may hold values from 0.25 to 4
- tokens: int32 [3, 256], replicated, may hold values from 0 to 4095
Outputs:
- forward: float32 [256, 32768], P('src', 'tgt')
- log_total: float32 [256], P('src')
Inputs may be any that keep to these rules, and one draw needn't show every extreme that they name: `transition`: every weight is positive.
All inputs are finite; a program needn't handle non-finite values.
Results may differ from a plain program's by a relative error of at most 0.00082.
Values may be sent and summed in bfloat16 or wider, within the bound.
A program may use at most 128 MiB of HBM per device.

v0:
```python
import jax
import jax.numpy as jnp
from jax import lax
from jax.sharding import PartitionSpec as P


def per_device(forward_init, transition, emission, tokens):
    n_src = lax.axis_size("src")
    n_tgt = lax.axis_size("tgt")
    src_index = lax.axis_index("src")
    seqs = forward_init.shape[0]
    share = seqs // n_src
    block = transition.shape[1]
    states = block * n_tgt
    span = states // n_src
    vocab_rows = emission.shape[0]
    steps = tokens.shape[0]
    local_ids = tokens - src_index * vocab_rows
    inside = (local_ids >= 0) & (local_ids < vocab_rows)
    picked = jnp.take(emission, jnp.clip(local_ids, 0, vocab_rows - 1), axis=0)
    masked = jnp.where(inside[:, :, None], picked.astype(jnp.float32), 0.0)
    rows_all = lax.psum(masked.astype(jnp.bfloat16), "src").astype(jnp.float32)
    current = forward_init.astype(jnp.bfloat16)
    log_sum = jnp.zeros((seqs,), jnp.float32)
    log_share = jnp.zeros((share,), jnp.float32)
    result = jnp.zeros((share, block), jnp.float32)
    for step in range(steps):
        final = step + 1 == steps
        partial_value = jnp.dot(current, transition, preferred_element_type=jnp.float32)
        summed = lax.psum(partial_value, "src")
        fresh = summed * rows_all[step] / states
        total = lax.psum(jnp.sum(fresh, axis=1), "tgt") / states
        log_sum = log_sum + jnp.log(total)
        normed = fresh / total[:, None]
        if not final:
            full = lax.all_gather(normed.astype(jnp.bfloat16), "tgt", axis=1, tiled=True)
            current = lax.dynamic_slice_in_dim(full, src_index * span, span, 1)
        else:
            result = lax.dynamic_slice_in_dim(normed, src_index * share, share, 0)
            log_share = lax.dynamic_slice_in_dim(log_sum, src_index * share, share, 0)
    return (result, log_share)


def solution(mesh):
    placed = (P(None, "src"), P("src", "tgt"), P("src", "tgt"), P())
    return jax.shard_map(
        per_device,
        mesh=mesh,
        in_specs=placed,
        out_specs=(P("src", "tgt"), P("src")),
        check_vma=False,
    )
```

profile of v0, /device:TPU:0, one launch (start us, length us, event | category | flops | bytes accessed | tf_op | source)
XLA Modules:
  0.0 870.6 jit_solution(6640386076629123048)
XLA Ops:
  7.2 0.8 compare_and_fusion
  8.1 0.7 copy-done
  8.8 3.6 gather_fusion
  12.3 3.0 select_convert_fusion
  15.4 13.6 %fusion.4 = f32[256,1024]{1,0:T(8,128)} fusion(bf16[8192,1024]{1,0:T(8,128)(2,1)} %param.5, f32[256,8192]{1,0:T(8,128)} %param.4), kind=kOutput, calls=%fused_computation.5 | convolution fusion | flops 4297064448 | bytes 26214400 | tf_op jit(solution)/shard_map/dot_general | solution.py:29
  29.1 40.0 %all-reduce.7.cloned.1.call-done = bf16[3,256,1024]{2,1,0:T(8,128)(2,1)} async-done(((bf16[3,256,1024]{2,1,0:T(8,128)(2,1)}), bf16[3,256,1024]{2,1,0:T(8,128)(2,1)}) %all-reduce.7.cloned.1.call-update) | async-done | bytes 1572880 | tf_op jit(solution)/shard_map/psum | solution.py:22
  69.1 3.5 convert_element_type.21
  72.6 43.6 %all-reduce.5.cloned.1.call-done = f32[256,1024]{1,0:T(8,128)} async-done(((f32[256,1024]{1,0:T(8,128)}), f32[256,1024]{1,0:T(8,128)}) %all-reduce.5.cloned.1.call-update) | async-done | bytes 1048592 | tf_op jit(solution)/shard_map/psum | solution.py:30
  116.2 1.7 fusion.12
  118.0 81.8 %psum.51 = f32[256]{0:T(256)S(1)} all-reduce(f32[256]{0:T(256)S(1)} %fusion.12), channel_id=1, replica_groups=mesh['src'=4,'tgt'=32] {'tgt'}, use_global_device_ids=true, to_apply=%region_3.4 | all-reduce | flops 256 | bytes 2048 | tf_op jit(solution)/shard_map/psum | solution.py:32
  199.7 2.6 divide_convert_fusion.1
  202.4 188.9 %all-gather.3.cloned.1.call-done = bf16[256,32768]{1,0:T(8,128)(2,1)} async-done(((bf16[256,1024]{1,0:T(8,128)(2,1)}), bf16[256,32768]{1,0:T(8,128)(2,1)}) %all-gather.3.cloned.1.call-update) | async-done | bytes 16777232 | tf_op jit(solution)/shard_map/all_gather | solution.py:36
  391.3 12.5 %fusion.2 = f32[256,1024]{1,0:T(8,128)} fusion(bf16[8192,1024]{1,0:T(8,128)(2,1)} %param.5, bf16[256,32768]{1,0:T(8,128)(2,1)} %all-gather.3.cloned.1.call-done, s32[]{:T(128)S(6)} %select_n.24), kind=kOutput, calls=%fused_computation.3 | convolution fusion | flops 4294967296 | bytes 22020100 | tf_op jit(solution)/shard_map/dot_general | solution.py:29
  403.9 43.5 %all-reduce.9.cloned.1.call-done = f32[256,1024]{1,0:T(8,128)} async-done(((f32[256,1024]{1,0:T(8,128)}), f32[256,1024]{1,0:T(8,128)}) %all-reduce.9.cloned.1.call-update) | async-done | bytes 1048592 | tf_op jit(solution)/shard_map/psum | solution.py:30
  447.4 1.7 fusion.13
  449.2 81.8 %psum.53 = f32[256]{0:T(256)S(1)} all-reduce(f32[256]{0:T(256)S(1)} %fusion.13), channel_id=1, replica_groups=mesh['src'=4,'tgt'=32] {'tgt'}, use_global_device_ids=true, to_apply=%region_6.7 | all-reduce | flops 256 | bytes 2048 | tf_op jit(solution)/shard_map/psum | solution.py:32
  530.9 2.6 divide_convert_fusion
  533.8 188.7 %all-gather.5.cloned.1.call-done = bf16[256,32768]{1,0:T(8,128)(2,1)} async-done(((bf16[256,1024]{1,0:T(8,128)(2,1)}), bf16[256,32768]{1,0:T(8,128)(2,1)}) %all-gather.5.cloned.1.call-update) | async-done | bytes 16777232 | tf_op jit(solution)/shard_map/all_gather | solution.py:36
  722.5 12.6 %fusion = f32[256,1024]{1,0:T(8,128)} fusion(bf16[8192,1024]{1,0:T(8,128)(2,1)} %param.5, bf16[256,32768]{1,0:T(8,128)(2,1)} %all-gather.5.cloned.1.call-done, s32[]{:T(128)S(6)} %select_n.24), kind=kOutput, calls=%fused_computation.1 | convolution fusion | flops 4294967296 | bytes 22020100 | tf_op jit(solution)/shard_map/dot_general | solution.py:29
  735.2 43.6 %all-reduce.11.cloned.1.call-done = f32[256,1024]{1,0:T(8,128)} async-done(((f32[256,1024]{1,0:T(8,128)}), f32[256,1024]{1,0:T(8,128)}) %all-reduce.11.cloned.1.call-update) | async-done | bytes 1048592 | tf_op jit(solution)/shard_map/psum | solution.py:30
  778.8 1.7 fusion.16
  780.5 81.8 %psum.55 = f32[256]{0:T(256)S(1)} all-reduce(f32[256]{0:T(256)S(1)} %get-tuple-element.2), channel_id=1, replica_groups=mesh['src'=4,'tgt'=32] {'tgt'}, use_global_device_ids=true, to_apply=%region_9.10 | all-reduce | flops 256 | bytes 2048 | tf_op jit(solution)/shard_map/psum | solution.py:32
  862.3 0.6 dynamic_slice.15
  862.9 0.8 dynamic-slice_divide_fusion
  (21 shorter events, 0.7 us)
Async XLA Ops:
  7.2 1.6 copy-start
  7.2 62.0 %all-reduce.7.cloned.1.call-start = ((), (), s32[]{:S(2)}) async-start(), calls=%async_computation.1 | async-start | bytes 3145728 | tf_op jit(solution)/shard_map/psum | solution.py:22
  15.4 100.9 %all-reduce.5.cloned.1.call-start = ((), (), s32[]{:S(2)}) async-start(), calls=%async_computation | async-start | bytes 2097152 | tf_op jit(solution)/shard_map/psum | solution.py:30
  29.1 362.3 %all-gather.3.cloned.1.call-start = ((), (), s32[]{:S(2)}) async-start(), calls=%async_computation.2 | async-start | bytes 17301504 | tf_op jit(solution)/shard_map/all_gather | solution.py:36
  202.4 245.1 %all-reduce.9.cloned.1.call-start = ((), (), s32[]{:S(2)}) async-start(), calls=%async_computation.3 | async-start | bytes 2097152 | tf_op jit(solution)/shard_map/psum | solution.py:30
  403.9 318.7 %all-gather.5.cloned.1.call-start = ((), (), s32[]{:S(2)}) async-start(), calls=%async_computation.4 | async-start | bytes 17301504 | tf_op jit(solution)/shard_map/all_gather | solution.py:36
  533.6 245.2 %all-reduce.11.cloned.1.call-start = ((), (), s32[]{:S(2)}) async-start(), calls=%async_computation.5 | async-start | bytes 2097152 | tf_op jit(solution)/shard_map/psum | solution.py:30
  722.5 141.2 %copy-start.1 = (bf16[1024,1024]{1,0:T(8,128)(2,1)S(1)}, bf16[1024,1024]{1,0:T(8,128)(2,1)}, u32[]{:S(2)}) copy-start(bf16[1024,1024]{1,0:T(8,128)(2,1)} %param.6) | copy-start | bytes 6291460
Sparse Core Ops, SparseCore 0:
  15.5 53.5 all-reduce.6
  71.7 44.5 all-reduce.4
  202.5 188.8 all-gather.2
  404.0 43.4 all-reduce.8
  533.7 188.8 all-gather.4
  735.3 43.3 all-reduce.10
where the time goes:
time: 871 us
  waiting for transfers between devices  548 us (63%)
  blocking collectives  245 us (28%)
  matrix products  38.8 us (4%)
  other arithmetic  18.5 us (2%)
  between operations  14.1 us (2%)
    all_gather x2, waiting for transfers between devices, per_device(): lax.all_gather(normed.astype(jnp.bfloat16), 'tgt', axis=1, tiled=True)  378 us
    psum x3, blocking collectives, per_device(): total = lax.psum(jnp.sum(fresh, axis=1), 'tgt') / states  245 us
    psum x3, waiting for transfers between devices, per_device(): summed = lax.psum(partial_value, 'src')  131 us
    psum x1, waiting for transfers between devices, per_device(): rows_all = lax.psum(masked.astype(jnp.bfloat16), 'src').astype(jnp.float32)  40 us
    dot_general x3, matrix products, per_device(): jnp.dot(current, transition, preferred_element_type=jnp.float32)  38.8 us
  transfers between devices with their start and end apart: 6, of which 6 were waited for; matrix products, arithmetic and copies ran while one was open for 2% of the time, Pallas kernels for 0%

commit v1 on v0

v1 whole, which is shorter than its diff:
```python
import functools

import jax
import jax.numpy as jnp
from jax import lax
from jax.experimental import pallas as pl
from jax.experimental.pallas import tpu as pltpu
from jax.sharding import PartitionSpec as P

MESH = pl.DeviceIdType.MESH
BLK = 1024
KB = 8
HALVES = 1
R = 64 // HALVES
ROWS = 4 * R
CA = 640
STEPS = 3
S = 32768.0


def place(q):
    return (q % 2) * 2 + q // 2


def kernel(tok, fwd, trans, emis, out, logs, tbuf, ebuf, stage, cur, acc, rs1, mid, rs2, erow, er1, emid, er2, emine, blk, tota, totb, fresh, lsum,
           ld_t, ld_f, ld_e, d_s, d_r, z_s, z_r, ed_s, ed_r, ez_s, ez_r, a_s, a_r, b_s, b_r, pa_s, pa_r, pb_s, pb_r, xa_s, xa_r, yb_s, yb_r, loc):
    s = lax.axis_index("src")
    t = lax.axis_index("tgt")
    zh, c = s // 2, s % 2
    y, zl, x = t // 8, (t // 4) % 2, t % 4
    is_self = s == y

    def dev(s_, y_, zl_, x_):
        return (s_, y_ * 8 + zl_ * 4 + x_)

    core = dev(zh * 2 + 1 - c, y, zl, x)
    zhp = dev((1 - zh) * 2 + c, y, zl, x)
    plane = [(dz, dx) for dz in range(2) for dx in range(4)]

    def in_plane(dz, dx):
        return dev(s, y, (zl + dz) % 2, (x + dx) % 4)

    def in_y(dy):
        return dev(s, (y + dy) % 4, zl, x)

    spread = [(o, dz) for dz in range(2) for o in range(4)]

    def dest_a(o, dz):
        return dev(y, (y + o) % 4, (zl + dz) % 2, x)

    def dest_b(o, dz):
        return dev(y, s, (zl + dz) % 2, (x + o) % 4)

    e_ld = pltpu.make_async_copy(emis, ebuf, ld_e)
    e_ld.start()

    def kb_rows(i):
        return pl.ds(pl.multiple_of(((i % 2) * 4 + i // 2) * BLK, BLK), BLK)

    def f_ld(i, slot):
        return pltpu.make_async_copy(fwd.at[:, kb_rows(i)], stage.at[slot], ld_f.at[slot])

    def t_ld(i):
        return pltpu.make_async_copy(trans.at[kb_rows(i)], tbuf.at[i], ld_t.at[i])

    for i in range(KB):
        if i < 2:
            f_ld(i, i).start()
        t_ld(i).start()

    barrier = pltpu.get_barrier_semaphore()

    def hello(d):
        pl.semaphore_signal(barrier, inc=1, device_id=d, device_id_type=MESH)

    hello(core)
    hello(zhp)
    n = 2
    for dz, dx in plane[1:]:
        hello(in_plane(dz, dx))
        n += 1
    for dy in range(1, 4):
        hello(in_y(dy))
        n += 1
    for o, dz in spread:
        src_a = dev((y + o) % 4, s, (zl + dz) % 2, x)
        src_b = dev(y, s, (zl + dz) % 2, (x + o) % 4)
        if (o, dz) == (0, 0):
            @pl.when(jnp.logical_not(is_self))
            def _():
                hello(src_a)
                hello(src_b)
        else:
            hello(src_a)
            hello(src_b)
            n += 2
    @pl.when(is_self)
    def _():
        pl.semaphore_wait(barrier, n)

    @pl.when(jnp.logical_not(is_self))
    def _():
        pl.semaphore_wait(barrier, n + 2)

    def remote(src, dst, ss, rs, d):
        return pltpu.make_async_remote_copy(src_ref=src, dst_ref=dst, send_sem=ss, recv_sem=rs, device_id=d, device_id_type=MESH)

    e_ld.wait()
    ecopies = []
    for k in range(STEPS):
        def pick(p, _):
            rows = pl.ds(pl.multiple_of(k * 256 + p * 64, 64), 64)
            ids = tok[rows, :]
            hot = jnp.concatenate(
                [jnp.where(ids == lax.broadcasted_iota(jnp.int32, (64, 128), 1) + v * 128, 1.0, 0.0) for v in range(8)], axis=1
            ).astype(jnp.bfloat16)
            erow[rows, :] = jnp.dot(hot, ebuf[...], preferred_element_type=jnp.float32).astype(jnp.bfloat16)
            return 0

        lax.fori_loop(0, 4, pick, 0)
        cp = remote(erow.at[pl.ds(pl.multiple_of(k * 256 + (1 - c) * 128, 128), 128)], er1.at[k], ed_s.at[k], ed_r.at[k], core)
        cp.start()
        ecopies.append(cp)

    ez = []
    for k in range(STEPS):
        ecopies[k].wait_recv()
        other = pl.multiple_of((1 - zh) * 64, 64)
        emid[k] = erow[pl.ds(pl.multiple_of(k * 256 + c * 128 + (1 - zh) * 64, 64), 64), :] + er1[k, pl.ds(other, 64), :]
        cp = remote(emid.at[k], er2.at[k], ez_s.at[k], ez_r.at[k], zhp)
        cp.start()
        ez.append(cp)
        ecopies.append(cp)
        emine[k] = erow[pl.ds(pl.multiple_of(k * 256 + c * 128 + zh * 64, 64), 64), :] + er1[k, pl.ds(pl.multiple_of(zh * 64, 64), 64), :]

    for i in range(KB):
        slot = i % 2
        f_ld(i, slot).wait()
        for q in range(4):
            for h in range(HALVES):
                cur[0, h, i, place(q) * R : (place(q) + 1) * R, :] = stage[slot, q * 64 + h * R : q * 64 + (h + 1) * R, :].astype(jnp.bfloat16)
        if i + 2 < KB:
            f_ld(i + 2, slot).start()
        t_ld(i).wait()
        for h in range(HALVES):
            part = jnp.dot(cur[0, h, i], tbuf[i], preferred_element_type=jnp.float32)
            if i == 0:
                acc[0, h] = part
            else:
                acc[0, h] += part

    drain = []

    def product(k, h):
        acc[k, h] = jnp.dot(cur[k, h, 0], tbuf[0], preferred_element_type=jnp.float32)

        def body(i, _):
            acc[k, h] += jnp.dot(cur[k, h, i], tbuf[i], preferred_element_type=jnp.float32)
            return 0

        lax.fori_loop(1, KB, body, 0)

    st = {}

    def core_start(k, h):
        cp = remote(acc.at[k, h, pl.ds(pl.multiple_of((1 - c) * 2 * R, 2 * R), 2 * R)], rs1.at[k, h], d_s.at[k, h], d_r.at[k, h], core)
        cp.start()
        st["d", k, h] = cp
        drain.append(cp)

    def core_end(k, h):
        st["d", k, h].wait_recv()
        mid[k, h] = acc[k, h, pl.ds(pl.multiple_of((c * 2 + 1 - zh) * R, R), R), :] + rs1[k, h, pl.ds(pl.multiple_of((1 - zh) * R, R), R), :]
        cp = remote(mid.at[k, h], rs2.at[k, h], z_s.at[k, h], z_r.at[k, h], zhp)
        cp.start()
        st["z", k, h] = cp
        drain.append(cp)
        fresh[h] = acc[k, h, pl.ds(pl.multiple_of((c * 2 + zh) * R, R), R), :] + rs1[k, h, pl.ds(pl.multiple_of(zh * R, R), R), :]

    def z_end(k, h):
        if h == 0:
            ez[k].wait_recv()
        st["z", k, h].wait_recv()
        rows = pl.ds(h * R, R)
        e = emine[k, rows, :].astype(jnp.float32) + er2[k, rows, :].astype(jnp.float32)
        v = (fresh[h] + rs2[k, h]) * e * (1.0 / S)
        fresh[h] = v
        lanes = v[:, 0:128]
        for g in range(1, 8):
            lanes = lanes + v[:, g * 128 : (g + 1) * 128]
        own = zl * 4 + x
        tota[k, h, own] = lanes
        for j, (dz, dx) in enumerate(plane[1:]):
            cp = remote(tota.at[k, h, own], tota.at[k, h, own], a_s.at[k, h, j], a_r.at[k, h], in_plane(dz, dx))
            cp.start()
            drain.append(cp)

    def a_end(k, h):
        pltpu.make_async_copy(tota.at[k, h, pl.ds(0, 7)], tota.at[k, h, pl.ds(0, 7)], a_r.at[k, h]).wait()
        v = tota[k, h, 0]
        for j in range(1, 8):
            v = v + tota[k, h, j]
        totb[k, h, y] = v
        for j in range(3):
            cp = remote(totb.at[k, h, y], totb.at[k, h, y], b_s.at[k, h, j], b_r.at[k, h], in_y(j + 1))
            cp.start()
            drain.append(cp)

    def b_end(k, h):
        pltpu.make_async_copy(totb.at[k, h, pl.ds(0, 3)], totb.at[k, h, pl.ds(0, 3)], b_r.at[k, h]).wait()
        v = totb[k, h, 0]
        for j in range(1, 4):
            v = v + totb[k, h, j]
        total = jnp.sum(v, axis=1, keepdims=True) * (1.0 / S)
        lg = jnp.broadcast_to(jnp.log(total), (R, 128))
        lsum[h] = lg if k == 0 else lsum[h] + lg
        normed = fresh[h] / total
        if k + 1 == STEPS:
            out[h * R : (h + 1) * R, :] = normed
            logs[h * R : (h + 1) * R, :] = lsum[h]
            return
        blk[k, h] = normed.astype(jnp.bfloat16)
        mine = pl.ds(pl.multiple_of(place(s) * R, R), R)
        home = x * 2 + zl
        for j, (o, dz) in enumerate(spread):
            for half, dest, ss, rs, cols in (
                (0, dest_a(o, dz), pa_s, pa_r, pl.ds(0, CA)),
                (1, dest_b(o, dz), pb_s, pb_r, pl.ds(CA, BLK - CA)),
            ):
                src = blk.at[k, h, :, cols]
                dst = cur.at[k + 1, h, home, mine, cols]
                cp = remote(src, dst, ss.at[k, h, j], rs.at[k, h], dest)
                if (o, dz) == (0, 0):
                    lcp = pltpu.make_async_copy(src, dst, rs.at[k, h])

                    @pl.when(is_self)
                    def _(lcp=lcp):
                        lcp.start()

                    @pl.when(jnp.logical_not(is_self))
                    def _(cp=cp):
                        cp.start()

                    st["self", k, h, half] = cp
                else:
                    cp.start()
                    drain.append(cp)

    def piece_a(k, h, xx, z):
        return cur.at[k + 1, h, xx * 2 + z, :, pl.ds(0, CA)]

    def piece_b(k, h, yy, z):
        return cur.at[k + 1, h, pl.ds(z * 4, 4), pl.ds(pl.multiple_of(place(yy) * R, R), R), pl.ds(CA, BLK - CA)]

    def ring_dev(axis, d):
        return dev(s, y, zl, (x + d + 4) % 4) if axis == 0 else dev(s, (y + d + 4) % 4, zl, x)

    def ring_start(k, h, axis):
        if axis == 0:
            whole = cur.at[k + 1, h, pl.ds(x * 2, 2), :, pl.ds(0, CA)]
            pltpu.make_async_copy(whole, whole, pa_r.at[k, h]).wait()
        else:
            whole = cur.at[k + 1, h, :, pl.ds(pl.multiple_of(place(y) * R, R), R), pl.ds(CA, BLK - CA)]
            pltpu.make_async_copy(whole, whole, pb_r.at[k, h]).wait()
        piece, me = (piece_a, x) if axis == 0 else (piece_b, y)
        ss, rs = (xa_s, xa_r) if axis == 0 else (yb_s, yb_r)
        for j, (d, z) in enumerate(((1, 0), (-1, 1), (1, 1), (-1, 0))):
            p = piece(k, h, me, z)
            cp = remote(p, p, ss.at[k, h, j], rs.at[k, h, j], ring_dev(axis, d))
            cp.start()
            st["r", k, h, axis, j] = cp
            drain.append(cp)

    def ring_pass(k, h, axis):
        piece, me = (piece_a, x) if axis == 0 else (piece_b, y)
        ss, rs = (xa_s, xa_r) if axis == 0 else (yb_s, yb_r)
        for j, (d, z) in ((0, (1, 0)), (1, (-1, 1))):
            st["r", k, h, axis, j].wait_recv()
            p = piece(k, h, (me - d + 4) % 4, z)
            cp = remote(p, p, ss.at[k, h, 4 + j], rs.at[k, h, 4 + j], ring_dev(axis, d))
            cp.start()
            st["r", k, h, axis, 4 + j] = cp
            drain.append(cp)

    def ring_end(k, h, axis):
        for j in range(2, 6):
            st["r", k, h, axis, j].wait_recv()

    hs = range(HALVES)
    for k in range(STEPS):
        if k == 0:
            for h in hs:
                core_start(k, h)
        for h in hs:
            core_end(k, h)
        for h in hs:
            z_end(k, h)
        for h in hs:
            a_end(k, h)
        for h in hs:
            b_end(k, h)
        if k + 1 < STEPS:
            for h in hs:
                for axis in range(2):
                    ring_start(k, h, axis)
                for axis in range(2):
                    ring_pass(k, h, axis)
            for h in hs:
                for axis in range(2):
                    ring_end(k, h, axis)
                product(k + 1, h)
                core_start(k + 1, h)

    for cp in drain:
        cp.wait_send()
    for cp in ecopies:
        cp.wait_send()

    @pl.when(jnp.logical_not(is_self))
    def _():
        for k in range(STEPS - 1):
            for h in hs:
                for half in range(2):
                    st["self", k, h, half].wait_send()


def per_device(forward_init, transition, emission, tokens):
    src = lax.axis_index("src")
    ids = tokens.reshape(STEPS, 2, 2, 64).transpose(0, 2, 1, 3).reshape(STEPS * 256, 1)
    ids = jnp.broadcast_to(ids - src * emission.shape[0], (STEPS * 256, 128))
    hbm = pl.BlockSpec(memory_space=pl.ANY)
    vmem = pl.BlockSpec(memory_space=pltpu.VMEM)
    V = pltpu.VMEM
    D = pltpu.SemaphoreType.DMA
    f32, bf16 = jnp.float32, jnp.bfloat16
    H = HALVES
    out, logs = pl.pallas_call(
        kernel,
        name="forward_window",
        out_shape=(jax.ShapeDtypeStruct((64, BLK), f32), jax.ShapeDtypeStruct((64, 128), f32)),
        in_specs=[vmem, hbm, hbm, hbm],
        out_specs=(vmem, vmem),
        scratch_shapes=[
            V((KB, BLK, BLK), bf16),
            V((1024, BLK), bf16),
            V((2, 256, BLK), f32),
            V((STEPS, H, KB, ROWS, BLK), bf16),
            V((STEPS, H, ROWS, BLK), f32),
            V((STEPS, H, 2 * R, BLK), f32),
            V((STEPS, H, R, BLK), f32),
            V((STEPS, H, R, BLK), f32),
            V((STEPS * 256, BLK), bf16),
            V((STEPS, 128, BLK), bf16),
            V((STEPS, 64, BLK), bf16),
            V((STEPS, 64, BLK), bf16),
            V((STEPS, 64, BLK), bf16),
            V((STEPS - 1, H, R, BLK), bf16),
            V((STEPS, H, 8, R, 128), f32),
            V((STEPS, H, 4, R, 128), f32),
            V((H, R, BLK), f32),
            V((H, R, 128), f32),
            D((KB,)), D((2,)), D,
            D((STEPS, H)), D((STEPS, H)), D((STEPS, H)), D((STEPS, H)),
            D((STEPS,)), D((STEPS,)), D((STEPS,)), D((STEPS,)),
            D((STEPS, H, 7)), D((STEPS, H)), D((STEPS, H, 3)), D((STEPS, H)),
            D((STEPS, H, 8)), D((STEPS, H)), D((STEPS, H, 8)), D((STEPS, H)),
            D((STEPS, H, 6)), D((STEPS, H, 6)), D((STEPS, H, 6)), D((STEPS, H, 6)),
            D,
        ],
        compiler_params=pltpu.CompilerParams(collective_id=0, has_side_effects=True, vmem_limit_bytes=58 * 2**20),
    )(ids, forward_init, transition, emission)
    return out, logs[:, 0]


def solution(mesh):
    placed = (P(None, "src"), P("src", "tgt"), P("src", "tgt"), P())
    return jax.shard_map(
        per_device,
        mesh=mesh,
        in_specs=placed,
        out_specs=(P("src", "tgt"), P("src")),
        check_vma=False,
    )
```

time: 871 us -> 183 us (0.21)
  waiting for transfers between devices: 548 us -> 0 us
  blocking collectives: 245 us -> 0 us
  Pallas kernels: 0 us -> 174 us
  matrix products: 38.8 us -> 0 us
  other arithmetic: 18.5 us -> 0.69 us
  between operations: 14.1 us -> 0.65 us
    all_gather x2 -> x0, waiting for transfers between devices: 378 us -> none  [per_device(): lax.all_gather(normed.astype(jnp.bfloat16), 'tgt', axis=1, tiled=True)]
    psum x3 -> x0, blocking collectives: 245 us -> none  [per_device(): total = lax.psum(jnp.sum(fresh, axis=1), 'tgt') / states]
    pallas_call x0 -> x1, Pallas kernels: none -> 174 us  [per_device(): pl.pallas_call(kernel, name='forward_window', out_shape=(jax.ShapeDtypeSt...]
    psum x4 -> x0, waiting for transfers between devices: 171 us -> none  [the longest x3 131 us: per_device(): summed = lax.psum(partial_value, 'src')]
    dot_general x3 -> x0, matrix products: 38.8 us -> none  [per_device(): jnp.dot(current, transition, preferred_element_type=jnp.float32)]
    convert_element_type x4 -> x0, other arithmetic: 11.6 us -> none  [the longest x2 6.47 us: per_device(): rows_all = lax.psum(masked.astype(jnp.bfloat16), 'src').astype(jnp.float32)]
  transfers between devices with their start and end apart: 6 -> 0, of which waited for: 6 -> 0; matrix products, arithmetic and copies ran while one was open for 2% -> 0% of each run, Pallas kernels for 0% -> 0%
where the time goes in v1:
time: 183 us; the launch traced here: 180 us
  Pallas kernels  174 us (95%)
  local copies, waits for them, and re-layouts  4.14 us (2%)
    pallas_call x1, Pallas kernels, per_device(): pl.pallas_call(kernel, name='forward_window', out_shape=(jax.ShapeDtypeSt...  174 us

profile of v1, /device:TPU:0, one launch (start us, length us, event | category | flops | bytes accessed | tf_op | source)
XLA Modules:
  0.0 179.9 jit_solution(8515298619895103573)
XLA Ops:
  0.6 0.7 broadcast_subtract_fusion
  1.3 0.1 sub.22
  1.4 0.1 sub.24
  1.5 0.9 broadcast_in_dim.2.tok
  2.4 174.4 %forward_window.1 = (f32[64,1024]{1,0:T(8,128)}, f32[64,128]{1,0:T(8,128)}) custom-call(s32[768,128]{1,0:T(8,128)} %broadcast_in_dim.2.tok, f32[256,8192]{1,0:T(8,128)} %fwd.1, bf16[8192,1024]{1,0:T(8,128)(2,1)} %trans.1, bf16[1024,1024]{1,0:T(8,128)(2,1)} %emis.1), custom_call_target="tpu_custom_call" | custom-call | tf_op jit(solution)/shard_map/forward_window/pallas_call | solution.py:337
  176.9 1.4 slice_reduce_fusion
  178.2 1.7 copy.10
  (1 shorter events, 0.0 us)

commit v2 on v0

v2 whole, which is shorter than its diff:
```python
import functools

import jax
import jax.numpy as jnp
from jax import lax
from jax.experimental import pallas as pl
from jax.experimental.pallas import tpu as pltpu
from jax.sharding import PartitionSpec as P

MESH = pl.DeviceIdType.MESH
BLK = 1024
KB = 8
HALVES = 2
R = 64 // HALVES
ROWS = 4 * R
CA = 512
STEPS = 3
AHEAD = 3
S = 32768.0


def place(q):
    return (q % 2) * 2 + q // 2


def kernel(tok, fwd, trans, emis, out, logs, tbuf, ebuf, stage, cur, acc, rs1, mid, rs2, erow, er1, emid, er2, blk, tota, totb, fresh, lsum, col,
           ld_t, ld_f, ld_e, d_s, d_r, z_s, z_r, ed_s, ed_r, ez_s, ez_r, a_s, a_r, b_s, b_r, t_s, t_r, g_s, g_r, xa_s, xa_r, yb_s, yb_r):
    s = lax.axis_index("src")
    t = lax.axis_index("tgt")
    zh, c = s // 2, s % 2
    y, zl, x = t // 8, (t // 4) % 2, t % 4
    is_self = s == y

    def dev(s_, y_, zl_, x_):
        return (s_, y_ * 8 + zl_ * 4 + x_)

    core = dev(zh * 2 + 1 - c, y, zl, x)
    zhp = dev((1 - zh) * 2 + c, y, zl, x)
    plane = [(dh, dz, dx) for dh in range(2) for dz in range(2) for dx in range(4)][1:]

    def in_plane(dh, dz, dx):
        return dev((zh + dh) % 2 * 2 + c, y, (zl + dz) % 2, (x + dx) % 4)

    def in_y(dy):
        return dev(s, (y + dy) % 4, zl, x)

    def in_x(dx):
        return dev(s, y, zl, (x + dx) % 4)

    def turned(dz):
        return dev(y, s, (zl + dz) % 2, x)

    def kb_rows(i):
        return pl.ds(pl.multiple_of(((i % 2) * 4 + i // 2) * BLK, BLK), BLK)

    def f_ld(i):
        return pltpu.make_async_copy(fwd.at[:, kb_rows(i)], stage.at[i], ld_f.at[i])

    def t_ld(i):
        return pltpu.make_async_copy(trans.at[kb_rows(i)], tbuf.at[i], ld_t.at[i])

    e_ld = pltpu.make_async_copy(emis, ebuf, ld_e)
    e_ld.start()

    barrier = pltpu.get_barrier_semaphore()

    def hello(d):
        pl.semaphore_signal(barrier, inc=1, device_id=d, device_id_type=MESH)

    hello(core)
    for p in plane:
        hello(in_plane(*p))
    for dy in range(1, 4):
        hello(in_y(dy))
    hello(turned(1))
    n = 1 + len(plane) + 3 + 1

    @pl.when(jnp.logical_not(is_self))
    def _():
        hello(turned(0))

    for i in range(AHEAD):
        f_ld(i).start()
        t_ld(i).start()

    def remote(src, dst, ss, rs, d):
        return pltpu.make_async_remote_copy(src_ref=src, dst_ref=dst, send_sem=ss, recv_sem=rs, device_id=d, device_id_type=MESH)

    drain = []

    def pick(k):
        ids = jnp.broadcast_to(tok[k : k + 1, :], (128, 256)).T - s * BLK
        ids = jnp.concatenate([ids[q * 64 : (q + 1) * 64, :] for q in (0, 2, 1, 3)], axis=0)
        lane = lax.broadcasted_iota(jnp.int32, (256, 128), 1)
        hot = jnp.concatenate([jnp.where(ids == lane + v * 128, 1.0, 0.0).astype(jnp.bfloat16) for v in range(8)], axis=1)
        erow[k] = jnp.dot(hot, ebuf[...], preferred_element_type=jnp.float32).astype(jnp.bfloat16)

    def own_rows(p, size):
        return pl.ds(pl.multiple_of(p * size, size), size)

    def part_rows(h, p, size):
        return pl.ds(pl.multiple_of(h * ROWS + p * size, size), size)

    est = {}

    def e_core_start(k):
        cp = remote(erow.at[k, own_rows(1 - c, 128)], er1.at[k], ed_s.at[k], ed_r.at[k], core)
        cp.start()
        est["d", k] = cp
        drain.append(cp)

    def e_z_start(k):
        est["d", k].wait_recv()
        for h in range(HALVES):
            for g in range(2):
                emid[k, h, g * R : (g + 1) * R, :] = erow[k, pl.ds(pl.multiple_of(c * 128 + g * 64 + h * R, R), R), :] + er1[k, g * 64 + h * R : g * 64 + (h + 1) * R, :]
            cp = remote(emid.at[k, h], er2.at[k, h], ez_s.at[k, h], ez_r.at[k, h], zhp)
            cp.start()
            est["z", k, h] = cp
            drain.append(cp)

    e_ld.wait()
    pick(0)

    @pl.when(is_self)
    def _():
        pl.semaphore_wait(barrier, n)

    @pl.when(jnp.logical_not(is_self))
    def _():
        pl.semaphore_wait(barrier, n + 1)

    e_core_start(0)
    e_z_start(0)

    acc[0] = jnp.zeros_like(acc[0])

    def first(i, _):
        f_ld(i).wait()
        for q in range(4):
            for h in range(HALVES):
                at = h * ROWS + place(q) * R
                cur[0, i, at : at + R, :] = stage[i, q * 64 + h * R : q * 64 + (h + 1) * R, :].astype(jnp.bfloat16)
        t_ld(i).wait()

        @pl.when(i + AHEAD < KB)
        def _():
            f_ld(i + AHEAD).start()
            t_ld(i + AHEAD).start()

        acc[0] += jnp.dot(cur[0, i], tbuf[i], preferred_element_type=jnp.float32)
        return 0

    lax.fori_loop(0, KB, first, 0)

    def product(k, h):
        def body(j, _):
            cols = pl.ds(pl.multiple_of(j * 512, 512), 512)
            v = jnp.dot(cur[k, 0, h * ROWS : (h + 1) * ROWS, :], tbuf[0, :, cols], preferred_element_type=jnp.float32)
            for i in range(1, KB):
                v = v + jnp.dot(cur[k, i, h * ROWS : (h + 1) * ROWS, :], tbuf[i, :, cols], preferred_element_type=jnp.float32)
            acc[k, h * ROWS : (h + 1) * ROWS, cols] = v
            return 0

        lax.fori_loop(0, BLK // 512, body, 0)

    st = {}

    def core_start(k, h):
        cp = remote(acc.at[k, part_rows(h, 1 - c, 2 * R)], rs1.at[k, h], d_s.at[k, h], d_r.at[k, h], core)
        cp.start()
        st["d", k, h] = cp
        drain.append(cp)

    def emission(k, h, g):
        rows = own_rows(g, R)
        return emid[k, h, rows, :].astype(jnp.float32) + er2[k, h, rows, :].astype(jnp.float32)

    def core_end(k, h):
        st["d", k, h].wait_recv()
        mid[k, h] = acc[k, part_rows(h, c, 2 * R), :] + rs1[k, h]
        est["z", k, h].wait_recv()
        parts = []
        for g in range(2):
            v = mid[k, h, g * R : (g + 1) * R, :] * emission(k, h, g)
            lanes = v[:, 0:128]
            for j in range(1, 8):
                lanes = lanes + v[:, j * 128 : (j + 1) * 128]
            parts.append(lanes)
            if R < 64:
                parts.append(jnp.zeros((64 - R, 128), jnp.float32))
        share = jnp.sum(jnp.concatenate(parts, axis=0).T, axis=0, keepdims=True)
        own = zh * 8 + zl * 4 + x
        tota[k, h, own] = jnp.broadcast_to(share, (8, 128))
        for j, p in enumerate(plane):
            cp = remote(tota.at[k, h, own], tota.at[k, h, own], a_s.at[k, h, j], a_r.at[k, h], in_plane(*p))
            cp.start()
            drain.append(cp)

    def z_start(k, h):
        cp = remote(mid.at[k, h, own_rows(1 - zh, R)], rs2.at[k, h], z_s.at[k, h], z_r.at[k, h], zhp)
        cp.start()
        st["z", k, h] = cp
        drain.append(cp)

    def a_end(k, h):
        pltpu.make_async_copy(tota.at[k, h, pl.ds(0, 15)], tota.at[k, h, pl.ds(0, 15)], a_r.at[k, h]).wait()
        v = tota[k, h, 0]
        for j in range(1, 16):
            v = v + tota[k, h, j]
        totb[k, h, y] = v
        for j in range(3):
            cp = remote(totb.at[k, h, y], totb.at[k, h, y], b_s.at[k, h, j], b_r.at[k, h], in_y(j + 1))
            cp.start()
            drain.append(cp)

    def z_end(k, h):
        st["z", k, h].wait_recv()
        fresh[k, h] = (mid[k, h, own_rows(zh, R), :] + rs2[k, h]) * emission(k, h, zh) * (1.0 / S)

    def b_end(k, h):
        pltpu.make_async_copy(totb.at[k, h, pl.ds(0, 3)], totb.at[k, h, pl.ds(0, 3)], b_r.at[k, h]).wait()
        v = totb[k, h, 0]
        for j in range(1, 4):
            v = v + totb[k, h, j]
        total = v * (1.0 / (S * S))
        col[h] = jnp.broadcast_to(total[0:1, :], (128, 128)).T
        normed = fresh[k, h] / col[h, pl.ds(pl.multiple_of(zh * 64, 64), R), 0:1]
        if k + 1 == STEPS:
            out[h * R : (h + 1) * R, :] = normed
        else:
            blk[k, h] = normed.astype(jnp.bfloat16)
            dst = cur.at[k + 1, x * 2 + zl, part_rows(h, place(s), R)]
            far = remote(blk.at[k, h], dst, t_s.at[k, h, 1], t_r.at[k, h], turned(1))
            far.start()
            drain.append(far)
            near = remote(blk.at[k, h], dst, t_s.at[k, h, 0], t_r.at[k, h], turned(0))
            here = pltpu.make_async_copy(blk.at[k, h], dst, t_r.at[k, h])

            @pl.when(is_self)
            def _():
                here.start()

            @pl.when(jnp.logical_not(is_self))
            def _():
                near.start()

            st["near", k, h] = near
        lsum[h] = jnp.log(total) if k == 0 else lsum[h] + jnp.log(total)

    def gather_start(k, h):
        rows = part_rows(h, place(y), R)
        whole = cur.at[k + 1, pl.ds(x * 2, 2), rows]
        pltpu.make_async_copy(whole, whole, t_r.at[k, h]).wait()
        for j in (0, 2, 1):
            for axis, cols, d in ((0, pl.ds(0, CA), in_y(j + 1)), (1, pl.ds(CA, BLK - CA), in_x(j + 1))):
                p = cur.at[k + 1, pl.ds(x * 2, 2), rows, cols]
                cp = remote(p, p, g_s.at[k, h, axis, j], g_r.at[k, h, axis], d)
                cp.start()
                drain.append(cp)

    def piece_a(k, h, xx, z):
        return cur.at[k + 1, xx * 2 + z, pl.ds(h * ROWS, ROWS), pl.ds(0, CA)]

    def piece_b(k, h, yy, z):
        return cur.at[k + 1, pl.ds(z * 4, 4), part_rows(h, place(yy), R), pl.ds(CA, BLK - CA)]

    def ring_dev(axis, d):
        return in_x(d + 4) if axis == 0 else in_y(d + 4)

    def ring_start(k, h, axis):
        if axis == 0:
            got = cur.at[k + 1, pl.ds(x * 2, 2), pl.ds(h * ROWS, 3 * R), pl.ds(0, CA)]
        else:
            got = cur.at[k + 1, pl.ds(0, 6), part_rows(h, place(y), R), pl.ds(CA, BLK - CA)]
        pltpu.make_async_copy(got, got, g_r.at[k, h, axis]).wait()
        piece, me = (piece_a, x) if axis == 0 else (piece_b, y)
        ss, rs = (xa_s, xa_r) if axis == 0 else (yb_s, yb_r)
        for j, (d, z) in enumerate(((1, 0), (-1, 1), (1, 1), (-1, 0))):
            p = piece(k, h, me, z)
            cp = remote(p, p, ss.at[k, h, j], rs.at[k, h, j], ring_dev(axis, d))
            cp.start()
            st["r", k, h, axis, j] = cp
            drain.append(cp)

    def ring_pass(k, h, axis):
        piece, me = (piece_a, x) if axis == 0 else (piece_b, y)
        ss, rs = (xa_s, xa_r) if axis == 0 else (yb_s, yb_r)
        for j, (d, z) in ((0, (1, 0)), (1, (-1, 1))):
            st["r", k, h, axis, j].wait_recv()
            p = piece(k, h, (me - d + 4) % 4, z)
            cp = remote(p, p, ss.at[k, h, 4 + j], rs.at[k, h, 4 + j], ring_dev(axis, d))
            cp.start()
            st["r", k, h, axis, 4 + j] = cp
            drain.append(cp)

    def ring_end(k, h, axis):
        for j in range(2, 6):
            st["r", k, h, axis, j].wait_recv()

    hs = range(HALVES)

    def both(f, k, h):
        for axis in range(2):
            f(k, h, axis)

    for h in hs:
        core_start(0, h)
    for h in hs:
        core_end(0, h)
    for h in hs:
        z_start(0, h)
    for h in hs:
        a_end(0, h)
    for h in hs:
        z_end(0, h)
        b_end(0, h)
    for k in range(STEPS - 1):
        for h in hs:
            gather_start(k, h)
        if k == 0:
            pick(1)
            e_core_start(1)
        both(ring_start, k, 0)
        both(ring_pass, k, 0)
        both(ring_start, k, 1)
        e_z_start(k + 1)
        if k == 0:
            pick(2)
            e_core_start(2)
        both(ring_end, k, 0)
        product(k + 1, 0)
        core_start(k + 1, 0)
        both(ring_pass, k, 1)
        core_end(k + 1, 0)
        z_start(k + 1, 0)
        both(ring_end, k, 1)
        product(k + 1, 1)
        core_start(k + 1, 1)
        a_end(k + 1, 0)
        core_end(k + 1, 1)
        z_end(k + 1, 0)
        z_start(k + 1, 1)
        a_end(k + 1, 1)
        b_end(k + 1, 0)
        z_end(k + 1, 1)
        b_end(k + 1, 1)

    parts = []
    for h in hs:
        v = lsum[h, 0:1, :]
        parts.append(jnp.where(zh == 0, v[:, 0:R], v[:, 64 : 64 + R]))
    logs[...] = parts[0] if HALVES == 1 else jnp.concatenate(parts, axis=1)

    for cp in drain:
        cp.wait_send()

    @pl.when(jnp.logical_not(is_self))
    def _():
        for k in range(STEPS - 1):
            for h in hs:
                st["near", k, h].wait_send()


def per_device(forward_init, transition, emission, tokens):
    hbm = pl.BlockSpec(memory_space=pl.ANY)
    vmem = pl.BlockSpec(memory_space=pltpu.VMEM)
    V = pltpu.VMEM
    D = pltpu.SemaphoreType.DMA
    f32, bf16 = jnp.float32, jnp.bfloat16
    H = HALVES
    out, logs = pl.pallas_call(
        kernel,
        name="forward_window",
        out_shape=(jax.ShapeDtypeStruct((64, BLK), f32), jax.ShapeDtypeStruct((1, 64), f32)),
        in_specs=[vmem, hbm, hbm, hbm],
        out_specs=(vmem, vmem),
        scratch_shapes=[
            V((KB, BLK, BLK), bf16),
            V((1024, BLK), bf16),
            V((KB, 256, BLK), f32),
            V((STEPS, KB, 256, BLK), bf16),
            V((STEPS, 256, BLK), f32),
            V((STEPS, H, 2 * R, BLK), f32),
            V((STEPS, H, 2 * R, BLK), f32),
            V((STEPS, H, R, BLK), f32),
            V((STEPS, 256, BLK), bf16),
            V((STEPS, 128, BLK), bf16),
            V((STEPS, H, 2 * R, BLK), bf16),
            V((STEPS, H, 2 * R, BLK), bf16),
            V((STEPS - 1, H, R, BLK), bf16),
            V((STEPS, H, 16, 8, 128), f32),
            V((STEPS, H, 4, 8, 128), f32),
            V((STEPS, H, R, BLK), f32),
            V((H, 8, 128), f32),
            V((H, 128, 128), f32),
            D((KB,)), D((KB,)), D,
            D((STEPS, H)), D((STEPS, H)), D((STEPS, H)), D((STEPS, H)),
            D((STEPS,)), D((STEPS,)), D((STEPS, H)), D((STEPS, H)),
            D((STEPS, H, 15)), D((STEPS, H)), D((STEPS, H, 3)), D((STEPS, H)),
            D((STEPS, H, 2)), D((STEPS, H)), D((STEPS, H, 2, 3)), D((STEPS, H, 2)),
            D((STEPS, H, 6)), D((STEPS, H, 6)), D((STEPS, H, 6)), D((STEPS, H, 6)),
        ],
        compiler_params=pltpu.CompilerParams(collective_id=0, has_side_effects=True, vmem_limit_bytes=60 * 2**20),
    )(tokens, forward_init, transition, emission)
    return out, logs.reshape(64)


def solution(mesh):
    placed = (P(None, "src"), P("src", "tgt"), P("src", "tgt"), P())
    return jax.shard_map(
        per_device,
        mesh=mesh,
        in_specs=placed,
        out_specs=(P("src", "tgt"), P("src")),
        check_vma=False,
    )
```

time: 871 us -> 124 us (0.14)
  waiting for transfers between devices: 548 us -> 0 us
  blocking collectives: 245 us -> 0 us
  Pallas kernels: 0 us -> 120 us
  matrix products: 38.8 us -> 0 us
  other arithmetic: 18.5 us -> 0 us
  between operations: 14.1 us -> 0.64 us
    all_gather x2 -> x0, waiting for transfers between devices: 378 us -> none  [per_device(): lax.all_gather(normed.astype(jnp.bfloat16), 'tgt', axis=1, tiled=True)]
    psum x3 -> x0, blocking collectives: 245 us -> none  [per_device(): total = lax.psum(jnp.sum(fresh, axis=1), 'tgt') / states]
    psum x4 -> x0, waiting for transfers between devices: 171 us -> none  [the longest x3 131 us: per_device(): summed = lax.psum(partial_value, 'src')]
    pallas_call x0 -> x1, Pallas kernels: none -> 120 us  [per_device(): pl.pallas_call(kernel, name='forward_window', out_shape=(jax.ShapeDtypeSt...]
    dot_general x3 -> x0, matrix products: 38.8 us -> none  [per_device(): jnp.dot(current, transition, preferred_element_type=jnp.float32)]
    convert_element_type x4 -> x0, other arithmetic: 11.6 us -> none  [the longest x2 6.47 us: per_device(): rows_all = lax.psum(masked.astype(jnp.bfloat16), 'src').astype(jnp.float32)]
  transfers between devices with their start and end apart: 6 -> 0, of which waited for: 6 -> 0; matrix products, arithmetic and copies ran while one was open for 2% -> 0% of each run, Pallas kernels for 0% -> 0%
where the time goes in v2:
time: 124 us; the launch traced here: 123 us
  Pallas kernels  120 us (97%)
  local copies, waits for them, and re-layouts  2.8 us (2%)
    pallas_call x1, Pallas kernels, per_device(): pl.pallas_call(kernel, name='forward_window', out_shape=(jax.ShapeDtypeSt...  120 us
    unnamed x2, local copies, waits for them, and re-layouts  2.8 us

profile of v2, /device:TPU:0, one launch (start us, length us, event | category | flops | bytes accessed | tf_op | source)
XLA Modules:
  0.0 123.4 jit_solution(6801271144078842519)
XLA Ops:
  0.6 120.0 %forward_window.1 = (f32[64,1024]{1,0:T(8,128)}, f32[1,64]{1,0:T(1,128)}) custom-call(s32[3,256]{1,0:T(4,128)} %tok.1, f32[256,8192]{1,0:T(8,128)} %fwd.1, bf16[8192,1024]{1,0:T(8,128)(2,1)} %trans.1, bf16[1024,1024]{1,0:T(8,128)(2,1)} %emis.1), custom_call_target="tpu_custom_call" | custom-call | tf_op jit(solution)/shard_map/forward_window/pallas_call | solution.py:372
  120.6 1.7 %copy.8 = f32[64,1024]{1,0:T(8,128)} copy(f32[64,1024]{1,0:T(8,128)} %get-tuple-element.8) | data formatting | bytes 524288
  122.3 1.1 copy.9

commit v3 on v2

--- a/solution.py
+++ b/solution.py
@@ -36,10 +36,14 @@
 
     core = dev(zh * 2 + 1 - c, y, zl, x)
     zhp = dev((1 - zh) * 2 + c, y, zl, x)
-    plane = [(dh, dz, dx) for dh in range(2) for dz in range(2) for dx in range(4)][1:]
-
-    def in_plane(dh, dz, dx):
-        return dev((zh + dh) % 2 * 2 + c, y, (zl + dz) % 2, (x + dx) % 4)
+    plane = [(dy, dx) for dy in range(4) for dx in range(4)][1:]
+    line = [(dh, dz) for dh in range(2) for dz in range(2)][1:]
+
+    def in_plane(dy, dx):
+        return dev(s, (y + dy) % 4, zl, (x + dx) % 4)
+
+    def in_z(dh, dz):
+        return dev((zh + dh) % 2 * 2 + c, y, (zl + dz) % 2, x)
 
     def in_y(dy):
         return dev(s, (y + dy) % 4, zl, x)
@@ -70,8 +74,8 @@
     hello(core)
     for p in plane:
         hello(in_plane(*p))
-    for dy in range(1, 4):
-        hello(in_y(dy))
+    for p in line:
+        hello(in_z(*p))
     hello(turned(1))
     n = 1 + len(plane) + 3 + 1
 
@@ -120,6 +124,9 @@
             drain.append(cp)
 
     e_ld.wait()
+    for i in range(AHEAD, KB):
+        f_ld(i).start()
+        t_ld(i).start()
     pick(0)
 
     @pl.when(is_self)
@@ -142,11 +149,6 @@
                 at = h * ROWS + place(q) * R
                 cur[0, i, at : at + R, :] = stage[i, q * 64 + h * R : q * 64 + (h + 1) * R, :].astype(jnp.bfloat16)
         t_ld(i).wait()
-
-        @pl.when(i + AHEAD < KB)
-        def _():
-            f_ld(i + AHEAD).start()
-            t_ld(i + AHEAD).start()
 
         acc[0] += jnp.dot(cur[0, i], tbuf[i], preferred_element_type=jnp.float32)
         return 0
@@ -164,6 +166,37 @@
 
         lax.fori_loop(0, BLK // 512, body, 0)
 
+    def product_early(k, h):
+        rows = slice(h * ROWS, (h + 1) * ROWS)
+
+        def body(j, _):
+            cols = pl.ds(pl.multiple_of(j * 512, 512), 512)
+            v = jnp.zeros((ROWS, 512), jnp.float32)
+            for d in (0, 1, 3):
+                for z in range(2):
+                    i = (x + d) % 4 * 2 + z
+                    v = v + jnp.dot(cur[k, i, rows, 0:CA], tbuf[i, 0:CA, cols], preferred_element_type=jnp.float32)
+            acc[k, rows, cols] = v
+            return 0
+
+        lax.fori_loop(0, BLK // 512, body, 0)
+
+    def product_late(k, h):
+        rows = slice(h * ROWS, (h + 1) * ROWS)
+
+        def body(j, _):
+            cols = pl.ds(pl.multiple_of(j * 512, 512), 512)
+            v = acc[k, rows, cols]
+            for z in range(2):
+                i = (x + 2) % 4 * 2 + z
+                v = v + jnp.dot(cur[k, i, rows, 0:CA], tbuf[i, 0:CA, cols], preferred_element_type=jnp.float32)
+            for i in range(KB):
+                v = v + jnp.dot(cur[k, i, rows, CA:BLK], tbuf[i, CA:BLK, cols], preferred_element_type=jnp.float32)
+            acc[k, rows, cols] = v
+            return 0
+
+        lax.fori_loop(0, BLK // 512, body, 0)
+
     st = {}
 
     def core_start(k, h):
@@ -179,6 +212,9 @@
     def core_end(k, h):
         st["d", k, h].wait_recv()
         mid[k, h] = acc[k, part_rows(h, c, 2 * R), :] + rs1[k, h]
+        z_start(k, h)
+
+    def share(k, h):
         est["z", k, h].wait_recv()
         parts = []
         for g in range(2):
@@ -189,9 +225,9 @@
             parts.append(lanes)
             if R < 64:
                 parts.append(jnp.zeros((64 - R, 128), jnp.float32))
-        share = jnp.sum(jnp.concatenate(parts, axis=0).T, axis=0, keepdims=True)
-        own = zh * 8 + zl * 4 + x
-        tota[k, h, own] = jnp.broadcast_to(share, (8, 128))
+        sums = jnp.sum(jnp.concatenate(parts, axis=0).T, axis=0, keepdims=True)
+        own = y * 4 + x
+        tota[k, h, own] = jnp.broadcast_to(sums, (8, 128))
         for j, p in enumerate(plane):
             cp = remote(tota.at[k, h, own], tota.at[k, h, own], a_s.at[k, h, j], a_r.at[k, h], in_plane(*p))
             cp.start()
@@ -208,9 +244,10 @@
         v = tota[k, h, 0]
         for j in range(1, 16):
             v = v + tota[k, h, j]
-        totb[k, h, y] = v
-        for j in range(3):
-            cp = remote(totb.at[k, h, y], totb.at[k, h, y], b_s.at[k, h, j], b_r.at[k, h], in_y(j + 1))
+        own = zh * 2 + zl
+        totb[k, h, own] = v
+        for j, p in enumerate(line):
+            cp = remote(totb.at[k, h, own], totb.at[k, h, own], b_s.at[k, h, j], b_r.at[k, h], in_z(*p))
             cp.start()
             drain.append(cp)
 
@@ -309,7 +346,7 @@
     for h in hs:
         core_end(0, h)
     for h in hs:
-        z_start(0, h)
+        share(0, h)
     for h in hs:
         a_end(0, h)
     for h in hs:
@@ -322,25 +359,32 @@
             pick(1)
             e_core_start(1)
         both(ring_start, k, 0)
+        if k == 0:
+            e_z_start(1)
         both(ring_pass, k, 0)
         both(ring_start, k, 1)
-        e_z_start(k + 1)
         if k == 0:
             pick(2)
             e_core_start(2)
+            e_z_start(2)
         both(ring_end, k, 0)
         product(k + 1, 0)
         core_start(k + 1, 0)
         both(ring_pass, k, 1)
         core_end(k + 1, 0)
-        z_start(k + 1, 0)
-        both(ring_end, k, 1)
-        product(k + 1, 1)
+        share(k + 1, 0)
+        for j in (2, 3):
+            st["r", k, 1, 0, j].wait_recv()
+        product_early(k + 1, 1)
+        for j in (4, 5):
+            st["r", k, 1, 0, j].wait_recv()
+        ring_end(k, 1, 1)
+        product_late(k + 1, 1)
         core_start(k + 1, 1)
         a_end(k + 1, 0)
         core_end(k + 1, 1)
+        share(k + 1, 1)
         z_end(k + 1, 0)
-        z_start(k + 1, 1)
         a_end(k + 1, 1)
         b_end(k + 1, 0)
         z_end(k + 1, 1)

time: 124 us -> 119 us (0.960)
  Pallas kernels: 120 us -> 115 us
    pallas_call x1, Pallas kernels: 120 us -> 115 us  [per_device(): pl.pallas_call(kernel, name='forward_window', out_shape=(jax.ShapeDtypeSt...]
where the time goes in v3:
time: 119 us; the launch traced here: 118 us
  Pallas kernels  115 us (97%)
  local copies, waits for them, and re-layouts  2.8 us (2%)
    pallas_call x1, Pallas kernels, per_device(): pl.pallas_call(kernel, name='forward_window', out_shape=(jax.ShapeDtypeSt...  115 us
    unnamed x2, local copies, waits for them, and re-layouts  2.8 us

profile of v3, /device:TPU:0, one launch (start us, length us, event | category | flops | bytes accessed | tf_op | source)
XLA Modules:
  0.0 118.3 jit_solution(4735487925943821615)
XLA Ops:
  0.6 114.9 %forward_window.1 = (f32[64,1024]{1,0:T(8,128)}, f32[1,64]{1,0:T(1,128)}) custom-call(s32[3,256]{1,0:T(4,128)} %tok.1, f32[256,8192]{1,0:T(8,128)} %fwd.1, bf16[8192,1024]{1,0:T(8,128)(2,1)} %trans.1, bf16[1024,1024]{1,0:T(8,128)(2,1)} %emis.1), custom_call_target="tpu_custom_call" | custom-call | tf_op jit(solution)/shard_map/forward_window/pallas_call | solution.py:416
  115.5 1.7 %copy.8 = f32[64,1024]{1,0:T(8,128)} copy(f32[64,1024]{1,0:T(8,128)} %get-tuple-element.8) | data formatting | bytes 524288
  117.2 1.1 copy.9

commit v4 on v3

--- a/solution.py
+++ b/solution.py
@@ -23,7 +23,7 @@
     return (q % 2) * 2 + q // 2
 
 
-def kernel(tok, fwd, trans, emis, out, logs, tbuf, ebuf, stage, cur, acc, rs1, mid, rs2, erow, er1, emid, er2, blk, tota, totb, fresh, lsum, col,
+def kernel(toks, fwd, trans, emis, outs, logs, tok, out, ld_k, o_s, tbuf, ebuf, stage, cur, acc, rs1, mid, rs2, erow, er1, emid, er2, blk, tota, totb, fresh, lsum, col,
            ld_t, ld_f, ld_e, d_s, d_r, z_s, z_r, ed_s, ed_r, ez_s, ez_r, a_s, a_r, b_s, b_r, t_s, t_r, g_s, g_r, xa_s, xa_r, yb_s, yb_r):
     s = lax.axis_index("src")
     t = lax.axis_index("tgt")
@@ -65,6 +65,8 @@
 
     e_ld = pltpu.make_async_copy(emis, ebuf, ld_e)
     e_ld.start()
+    k_ld = pltpu.make_async_copy(toks, tok, ld_k)
+    k_ld.start()
 
     barrier = pltpu.get_barrier_semaphore()
 
@@ -123,6 +125,7 @@
             est["z", k, h] = cp
             drain.append(cp)
 
+    k_ld.wait()
     e_ld.wait()
     for i in range(AHEAD, KB):
         f_ld(i).start()
@@ -265,6 +268,7 @@
         normed = fresh[k, h] / col[h, pl.ds(pl.multiple_of(zh * 64, 64), R), 0:1]
         if k + 1 == STEPS:
             out[h * R : (h + 1) * R, :] = normed
+            pltpu.make_async_copy(out.at[pl.ds(h * R, R)], outs.at[pl.ds(h * R, R)], o_s.at[h]).start()
         else:
             blk[k, h] = normed.astype(jnp.bfloat16)
             dst = cur.at[k + 1, x * 2 + zl, part_rows(h, place(s), R)]
@@ -398,6 +402,8 @@
 
     for cp in drain:
         cp.wait_send()
+    for h in hs:
+        pltpu.make_async_copy(out.at[pl.ds(h * R, R)], outs.at[pl.ds(h * R, R)], o_s.at[h]).wait()
 
     @pl.when(jnp.logical_not(is_self))
     def _():
@@ -417,9 +423,12 @@
         kernel,
         name="forward_window",
         out_shape=(jax.ShapeDtypeStruct((64, BLK), f32), jax.ShapeDtypeStruct((1, 64), f32)),
-        in_specs=[vmem, hbm, hbm, hbm],
-        out_specs=(vmem, vmem),
+        in_specs=[hbm, hbm, hbm, hbm],
+        out_specs=(hbm, vmem),
         scratch_shapes=[
+            V((STEPS, 256), jnp.int32),
+            V((64, BLK), f32),
+            D, D((H,)),
             V((KB, BLK, BLK), bf16),
             V((1024, BLK), bf16),
             V((KB, 256, BLK), f32),

time: 119 us -> 118 us (level)
  no operation moved by 1% of the time
where the time goes in v4:
time: 118 us
  Pallas kernels  114 us (97%)
  local copies, waits for them, and re-layouts  2.8 us (2%)
    pallas_call x1, Pallas kernels, per_device(): pl.pallas_call(kernel, name='forward_window', out_shape=(jax.ShapeDtypeSt...  114 us
    unnamed x2, local copies, waits for them, and re-layouts  2.8 us

profile of v4, /device:TPU:0, one launch (start us, length us, event | category | flops | bytes accessed | tf_op | source)
XLA Modules:
  0.0 117.9 jit_solution(18076487178778076880)
XLA Ops:
  0.6 114.5 %forward_window.1 = (f32[64,1024]{1,0:T(8,128)}, f32[1,64]{1,0:T(1,128)}) custom-call(s32[3,256]{1,0:T(4,128)} %toks.1, f32[256,8192]{1,0:T(8,128)} %fwd.1, bf16[8192,1024]{1,0:T(8,128)(2,1)} %trans.1, bf16[1024,1024]{1,0:T(8,128)(2,1)} %emis.1), custom_call_target="tpu_custom_call" | custom-call | tf_op jit(solution)/shard_map/forward_window/pallas_call | solution.py:422
  115.1 1.7 %copy.8 = f32[64,1024]{1,0:T(8,128)} copy(f32[64,1024]{1,0:T(8,128)} %get-tuple-element.8) | data formatting | bytes 524288
  116.8 1.1 copy.9
